TPU v7x, 512 devices: a whole 4x8x8 slice. The times are simulated.
512 devices in a mesh: section: 8 (over y), replica: 64 (over z, x, core).
Axes of the slice: x: 4, y: 8, z: 8, core: 2. Of those that a mesh axis runs over, the one named last changes fastest.
Arguments:
- coords_in: bfloat16 [2, 8192, 512], P(None, 'replica'), may hold values from -6 to 6
- token_rows: bfloat16 [2, 8192, 2048], P(None, 'replica'), may hold values from -16 to 16
- cotangent: bfloat16 [2, 8192, 512], P(None, 'replica'), may hold values from -6 to 6
- subspace_basis: bfloat16 [512, 2048], replicated, may hold values from -0.25 to 0.25
- norm_gain: float32 [8, 2048], P('section'), may hold values from 0.5 to 1.5
- gate_weight: float32 [8, 2048, 256], P('section', 'replica'), may hold values from -0.125 to 0.125
- up_weight: bfloat16 [8, 2048, 256], P('section', 'replica'), may hold values from -0.125 to 0.125
- down_weight: float32 [8, 256, 512], P('section', 'replica'), may hold values from -0.375 to 0.375
- gate_moment: float32 [8, 2048, 256], P('section', 'replica'), may hold values from -0.625 to 0.625
- gate_second: float32 [8, 2048, 256], P('section', 'replica'), may hold values from 0.01 to 0.1
- down_moment: float32 [8, 256, 512], P('section', 'replica'), may hold values from -0.625 to 0.625
- down_second: float32 [8, 256, 512], P('section', 'replica'), may hold values from 0.01 to 0.1
Outputs:
- section_coords: bfloat16 [8, 2, 8192, 512], P('section', None, 'replica')
- coord_grads: bfloat16 [8, 2, 8192, 512], P('section', None, 'replica')
- gate_new: float32 [8, 2048, 256], P('section', 'replica')
- gate_moment_new: float32 [8, 2048, 256], P('section', 'replica')
- gate_second_new: float32 [8, 2048, 256], P('section', 'replica')
- down_new: float32 [8, 256, 512], P('section', 'replica')
- down_moment_new: float32 [8, 256, 512], P('section', 'replica')
- down_second_new: float32 [8, 256, 512], P('section', 'replica')
All inputs are finite; a program needn't handle non-finite values.
Results may differ from a plain program's by a relative error of at most 0.03.
Values may be sent and summed in bfloat16 or wider, within the bound.
A program may use at most 64 MiB of HBM per device.

v0:
```python
import math
import jax
import jax.numpy as jnp
from jax import lax
from jax.sharding import PartitionSpec as P

epsilon = 1e-06
learn_rate = 0.001
decay_first = 0.9
decay_second = 0.95
step_count = 10
adam_floor = 1e-08


def from_behind(value, axis, steps):
    count = lax.axis_size(axis)
    first, last = (max(0, -steps), min(count, count - steps))
    return lax.ppermute(value, axis, [(source, source + steps) for source in range(first, last)])


def contract_last(left, right):
    return lax.dot_general(
        left, right, (((1,), (1,)), ((), ())), preferred_element_type=jnp.float32
    )


def contract_first(left, right):
    return lax.dot_general(
        left, right, (((0,), (0,)), ((), ())), preferred_element_type=jnp.float32
    )


def silu_parts(gate_value):
    sigma = jax.nn.sigmoid(gate_value)
    return (gate_value * sigma, sigma * (1.0 + gate_value * (1.0 - sigma)))


def section_forward(coords, token_block, subspace_basis, gain_row, w_gate, w_up, w_down):
    expanded = jnp.dot(
        coords, subspace_basis, preferred_element_type=jnp.float32
    ) + token_block.astype(jnp.float32)
    inverse = lax.rsqrt(jnp.mean(expanded * expanded, axis=1, keepdims=True) + epsilon)
    normed = (expanded * inverse * gain_row).astype(jnp.bfloat16)
    gate_value = jnp.dot(normed, w_gate, preferred_element_type=jnp.float32)
    up_value = jnp.dot(normed, w_up, preferred_element_type=jnp.float32)
    active, slope_value = silu_parts(gate_value)
    hidden = (active * up_value).astype(jnp.bfloat16)
    output = (
        coords.astype(jnp.float32) + jnp.dot(hidden, w_down, preferred_element_type=jnp.float32)
    ).astype(jnp.bfloat16)
    return (output, (expanded, inverse, normed, gate_value, up_value, hidden))


def section_backward(next_grad, saved, subspace_basis, gain_row, w_gate, w_up, w_down):
    expanded, inverse, normed, gate_value, up_value, hidden = saved
    hidden_grad = contract_last(next_grad, w_down)
    down_term = contract_first(hidden, next_grad)
    active, slope_value = silu_parts(gate_value)
    gate_grad = (hidden_grad * up_value * slope_value).astype(jnp.bfloat16)
    up_grad = (hidden_grad * active).astype(jnp.bfloat16)
    gate_term = contract_first(normed, gate_grad)
    normed_grad = contract_last(gate_grad, w_gate) + contract_last(up_grad, w_up)
    scaled = normed_grad * gain_row
    centred = expanded * inverse
    expanded_grad = (
        inverse * (scaled - centred * jnp.mean(scaled * centred, axis=1, keepdims=True))
    ).astype(jnp.bfloat16)
    coord_grad = (
        next_grad.astype(jnp.float32) + contract_last(expanded_grad, subspace_basis)
    ).astype(jnp.bfloat16)
    return (coord_grad, gate_term, down_term)


def adam_update(weight_now, moment, second, gradient):
    moment_new = decay_first * moment + (1.0 - decay_first) * gradient
    second_new = decay_second * second + (1.0 - decay_second) * gradient * gradient
    update = (
        learn_rate
        * (moment_new / (1.0 - decay_first**step_count))
        / (jnp.sqrt(second_new / (1.0 - decay_second**step_count)) + adam_floor)
    )
    return (weight_now - update, moment_new, second_new)


def per_device(
    coords_in,
    token_rows,
    cotangent,
    subspace_basis,
    norm_gain,
    gate_weight,
    up_weight,
    down_weight,
    gate_moment,
    gate_second,
    down_moment,
    down_second,
):
    batches = coords_in.shape[0]
    rows_dev = coords_in.shape[1]
    coord_width = subspace_basis.shape[0]
    model_width = subspace_basis.shape[1]
    sections = lax.axis_size("section")
    section_index = lax.axis_index("section")
    tick_count = sections + batches - 1
    w_gate, w_up, w_down = (
        lax.all_gather(gate_weight[0].astype(jnp.bfloat16), "replica", axis=0, tiled=True),
        lax.all_gather(up_weight[0], "replica", axis=0, tiled=True),
        lax.all_gather(down_weight[0].astype(jnp.bfloat16), "replica", axis=0, tiled=True),
    )
    hidden_width = w_gate.shape[1]
    weights = (subspace_basis, norm_gain, w_gate, w_up, w_down)
    kept_buffers = (jnp.zeros((batches, rows_dev, coord_width), jnp.bfloat16),)
    produced = jnp.zeros((batches, rows_dev, coord_width), jnp.bfloat16)
    blank = jnp.zeros((rows_dev, coord_width), jnp.bfloat16)

    def forward_tick(carry, tick_now):
        incoming, produced, kept_buffers = carry
        batch_now = tick_now - section_index
        is_live = (batch_now >= 0) & (batch_now < batches)
        slot_index = jnp.clip(batch_now, 0, batches - 1)
        source = jnp.where(
            section_index == 0, lax.dynamic_index_in_dim(coords_in, slot_index, 0, False), incoming
        )
        token_block = lax.dynamic_index_in_dim(token_rows, slot_index, 0, False)

        def forward_run_layer(buffers):
            produced_now, kept_now = buffers
            output, saved = section_forward(source, token_block, *weights)
            produced_now = lax.dynamic_update_index_in_dim(produced_now, output, slot_index, 0)
            entries = (source,)
            kept_now = tuple(
                (
                    lax.dynamic_update_index_in_dim(buffer, item, slot_index, 0)
                    for buffer, item in zip(kept_now, entries)
                )
            )
            return (produced_now, kept_now)

        produced, kept_buffers = lax.cond(
            is_live, forward_run_layer, lambda unchanged: unchanged, (produced, kept_buffers)
        )
        outgoing = lax.dynamic_index_in_dim(produced, slot_index, 0, False)
        incoming = from_behind(outgoing, "section", 1)
        return ((incoming, produced, kept_buffers), None)

    (incoming, produced, kept_buffers), unused = lax.scan(
        forward_tick, (blank, produced, kept_buffers), jnp.arange(tick_count, dtype=jnp.int32)
    )

    def backward_tick(carry, tick_now):
        incoming, returned, gate_acc, down_acc = carry
        batch_now = tick_now - (sections - 1 - section_index)
        is_live = (batch_now >= 0) & (batch_now < batches)
        slot_index = jnp.clip(batch_now, 0, batches - 1)
        next_grad = jnp.where(
            section_index == sections - 1,
            lax.dynamic_index_in_dim(cotangent, slot_index, 0, False),
            incoming,
        )

        def backward_run_layer(buffers):
            returned_now, gate_now, down_now = buffers
            source = lax.dynamic_index_in_dim(kept_buffers[0], slot_index, 0, False)
            token_block = lax.dynamic_index_in_dim(token_rows, slot_index, 0, False)
            saved = section_forward(source, token_block, *weights)[1]
            coord_grad, gate_term, down_term = section_backward(next_grad, saved, *weights)
            returned_now = lax.dynamic_update_index_in_dim(returned_now, coord_grad, slot_index, 0)
            return (returned_now, gate_now + gate_term, down_now + down_term)

        returned, gate_acc, down_acc = lax.cond(
            is_live, backward_run_layer, lambda unchanged: unchanged, (returned, gate_acc, down_acc)
        )
        outgoing = lax.dynamic_index_in_dim(returned, slot_index, 0, False)
        incoming = from_behind(outgoing, "section", -1)
        return ((incoming, returned, gate_acc, down_acc), None)

    returned = jnp.zeros((batches, rows_dev, coord_width), jnp.bfloat16)
    gate_zero = jnp.zeros((model_width, hidden_width), jnp.float32)
    down_zero = jnp.zeros((hidden_width, coord_width), jnp.float32)
    (incoming, returned, gate_acc, down_acc), unused = lax.scan(
        backward_tick,
        (blank, returned, gate_zero, down_zero),
        jnp.arange(tick_count, dtype=jnp.int32),
    )
    gate_share, down_share = (
        lax.psum_scatter(gate_acc, "replica", scatter_dimension=0, tiled=True),
        lax.psum_scatter(down_acc, "replica", scatter_dimension=0, tiled=True),
    )
    grad_scale = 1.0 / math.sqrt(batches * rows_dev * lax.axis_size("replica"))
    gate_new, gate_moment_new, gate_second_new = adam_update(
        gate_weight[0], gate_moment[0], gate_second[0], gate_share * grad_scale
    )
    down_new, down_moment_new, down_second_new = adam_update(
        down_weight[0], down_moment[0], down_second[0], down_share * grad_scale
    )
    return (
        produced[None],
        returned[None],
        gate_new[None],
        gate_moment_new[None],
        gate_second_new[None],
        down_new[None],
        down_moment_new[None],
        down_second_new[None],
    )


def solution(mesh):
    placed = (
        P(None, "replica", None),
        P(None, "replica", None),
        P(None, "replica", None),
        P(),
        P("section", None),
        P("section", "replica", None),
        P("section", "replica", None),
        P("section", "replica", None),
        P("section", "replica", None),
        P("section", "replica", None),
        P("section", "replica", None),
        P("section", "replica", None),
    )
    return jax.shard_map(
        per_device,
        mesh=mesh,
        in_specs=placed,
        out_specs=(
            P("section", None, "replica", None),
            P("section", None, "replica", None),
            P("section", "replica", None),
            P("section", "replica", None),
            P("section", "replica", None),
            P("section", "replica", None),
            P("section", "replica", None),
            P("section", "replica", None),
        ),
        check_vma=False,
    )
```

profile of v0, /device:TPU:8, one launch (start us, length us, event | category | flops | bytes accessed | tf_op | source)
XLA Modules:
  0.0 806.3 jit_solution(16639715585179184832)
XLA Ops:
  10.1 50.3 %all-gather.1 = bf16[64,4,512]{2,1,0:T(4,128)(2,1)S(1)} all-gather(bf16[1,4,512]{2,1,0:T(4,128)(2,1)S(1)} %fusion.30), channel_id=1, replica_groups=mesh['section'=8,'replica'=64] {'replica'}, dimensions={0}, use_global_device_ids=true | all-gather | bytes 266240 | tf_op jit(solution)/shard_map/all_gather | solution.py:109
  60.4 38.6 %all-gather.5.cloned.1.call-done = bf16[2048,256]{1,0:T(8,128)(2,1)} async-done(((bf16[32,256]{1,0:T(8,128)(2,1)}), bf16[2048,256]{1,0:T(8,128)(2,1)}) %all-gather.5.cloned.1.call-update) | async-done | bytes 1048592 | tf_op jit(solution)/shard_map/all_gather | solution.py:107
  99.0 83.1 %all-gather.7.cloned.1.call-done = bf16[1,2048,256]{2,1,0:T(8,128)(2,1)} async-done(((bf16[1,32,256]{2,1,0:T(8,128)(2,1)}), bf16[1,2048,256]{2,1,0:T(8,128)(2,1)}) %all-gather.7.cloned.1.call-update) | async-done | bytes 1048592 | tf_op jit(solution)/shard_map/all_gather | solution.py:108
  182.9 107.2 %while.33 = (s32[]{:T(128)}, bf16[128,512]{1,0:T(8,128)(2,1)S(1)}, bf16[2,128,512]{2,1,0:T(8,128)(2,1)}, bf16[2,128,512]{2,1,0:T(8,128)(2,1)S(1)}, s32[9]{0:T(12...) while((s32[]{:T(128)}, bf16[128,512]{1,0:T(8,128)(2,1)S(1)}, ...), condition=%wide.region_4.5_spmd, body=%wide.region_0.4_spmd.sunk | while | flops 573505664 | bytes 18533412 | solution.py:147
  185.1 3.4 collective-permute-start
  188.5 7.3 collective-permute-done
  197.1 5.0 conditional.4
  205.0 5.1 collective-permute-done
  211.3 5.0 conditional.4
  219.5 4.6 collective-permute-done
  226.3 7.2 collective-permute-start
  233.6 2.5 collective-permute-done
  238.2 4.4 collective-permute-start
  247.3 6.9 collective-permute-start
  258.9 4.4 collective-permute-start
  263.3 2.5 collective-permute-done
  268.0 9.3 %collective-permute-start = (bf16[128,512]{1,0:T(8,128)(2,1)S(1)}, bf16[128,512]{1,0:T(8,128)(2,1)S(1)}, u32[]{:S(2)}, u32[]{:S(2)}) collective-permute-start(bf16[128,512]{1,0:T(8,128)(2,1)S(1)} %dynamic-slice_bitcast_fusion.4), channel_id=1, source_target_pairs={{0,64},{64,128},{128,192},{192,256},{256,320},{320,384},{384,448},... | collective-permute-start | bytes 393224 | tf_op jit(solution)/shard_map/while/body/eval_jaxpr/ppermute | solution.py:18
  282.0 5.6 collective-permute-start
  292.4 166.3 %while.34 = (s32[]{:T(128)}, bf16[128,512]{1,0:T(8,128)(2,1)S(1)}, bf16[2,128,512]{2,1,0:T(8,128)(2,1)}, f32[2048,256]{1,0:T(8,128)}, f32[256,512]{1,0:T(8,128)S...) while((s32[]{:T(128)}, bf16[128,512]{1,0:T(8,128)(2,1)S(1)}, ...), condition=%wide.region_10.11_spmd, body=%wide.region_5.10_spmd.sunk | while | flops 1281163392 | bytes 53303908 | solution.py:181
  296.5 6.7 collective-permute-done.1
  307.4 6.6 collective-permute-done.1
  318.1 8.6 %collective-permute-done.1 = bf16[128,512]{1,0:T(8,128)(2,1)S(1)} collective-permute-done((bf16[128,512]{1,0:T(8,128)(2,1)S(1)}, bf16[128,512]{1,0:T(8,128)(2,1)S(1)}, u32[]{:S(2)}, u32[]{:S(2)}) %collective-permute-start.1) | collective-permute-done | bytes 131104 | tf_op jit(solution)/shard_map/while/body/eval_jaxpr/ppermute | solution.py:18
  330.9 6.1 collective-permute-done.1
  341.2 5.2 collective-permute-done.1
  350.9 56.1 %collective-permute-done.1 = bf16[128,512]{1,0:T(8,128)(2,1)S(1)} collective-permute-done((bf16[128,512]{1,0:T(8,128)(2,1)S(1)}, bf16[128,512]{1,0:T(8,128)(2,1)S(1)}, u32[]{:S(2)}, u32[]{:S(2)}) %collective-permute-start.1) | collective-permute-done | bytes 131104 | tf_op jit(solution)/shard_map/while/body/eval_jaxpr/ppermute | solution.py:18
  408.2 8.6 %conditional.5 = ((bf16[2,128,512]{2,1,0:T(8,128)(2,1)}, f32[2048,256]{1,0:T(8,128)}, f32[256,512]{1,0:T(8,128)S(1)})) conditional(s32[]{:T(128)} %convert_element_type.126, (bf16[2,128,512]{2,1,0:T(8,128)(2,1)}, f32[2048,256]{1,0:T(8,128)}, f32[256,512]{1,0:T(8,128)S(1)}) %tuple.84, (pred[]{:T(512)}, bf16[2,128,512]{2,1,0:T(8,128)(2,1)}, s32[]{:T(128)}, ...), branch_computations={%region_6.6_spmd, %region_7.9_spmd} | conditional | flops 1281163392 | bytes 52517052 | solution.py:171
  419.7 6.1 collective-permute-done.1
  427.1 8.6 %conditional.5 = ((bf16[2,128,512]{2,1,0:T(8,128)(2,1)}, f32[2048,256]{1,0:T(8,128)}, f32[256,512]{1,0:T(8,128)S(1)})) conditional(s32[]{:T(128)} %convert_element_type.126, (bf16[2,128,512]{2,1,0:T(8,128)(2,1)}, f32[2048,256]{1,0:T(8,128)}, f32[256,512]{1,0:T(8,128)S(1)}) %tuple.84, (pred[]{:T(512)}, bf16[2,128,512]{2,1,0:T(8,128)(2,1)}, s32[]{:T(128)}, ...), branch_computations={%region_6.6_spmd, %region_7.9_spmd} | conditional | flops 1281163392 | bytes 52517052 | solution.py:171
  438.6 4.9 collective-permute-done.1
  445.7 10.5 %collective-permute-start.1 = (bf16[128,512]{1,0:T(8,128)(2,1)S(1)}, bf16[128,512]{1,0:T(8,128)(2,1)S(1)}, u32[]{:S(2)}, u32[]{:S(2)}) collective-permute-start(bf16[128,512]{1,0:T(8,128)(2,1)S(1)} %dynamic-slice_bitcast_fusion.5), channel_id=1, source_target_pairs={{64,0},{128,64},{192,128},{256,192},{320,256},{384,320},{448,384},... | collective-permute-start | bytes 393224 | tf_op jit(solution)/shard_map/while/body/eval_jaxpr/ppermute | solution.py:18
  462.1 185.5 %all-reduce.3.cloned.1.call-done = f32[256,512]{1,0:T(8,128)} async-done(((f32[256,512]{1,0:T(8,128)}), f32[256,512]{1,0:T(8,128)}) %all-reduce.3.cloned.1.call-update) | async-done | bytes 524304
  648.9 149.5 %reduce-scatter.2.cloned.1.call-done = f32[32,256]{1,0:T(8,128)} async-done(((f32[2048,256]{1,0:T(8,128)}), f32[32,256]{1,0:T(8,128)}) %reduce-scatter.2.cloned.1.call-update) | async-done | bytes 32784 | tf_op jit(solution)/shard_map/reduce_scatter | solution.py:187
  (170 shorter events, 97.9 us)
Async XLA Ops:
  7.2 91.8 %all-gather.5.cloned.1.call-start = ((), (), s32[]{:S(2)}) async-start(), calls=%async_computation.1 | async-start | bytes 1064960 | tf_op jit(solution)/shard_map/all_gather | solution.py:107
  8.6 173.5 %all-gather.7.cloned.1.call-start = ((), (), s32[]{:S(2)}) async-start(), calls=%async_computation.3 | async-start | bytes 1064960 | tf_op jit(solution)/shard_map/all_gather | solution.py:108
  9.4 638.2 %all-reduce.3.cloned.1.call-start = ((), (), s32[]{:S(2)}) async-start(), calls=%async_computation.4 | async-start | bytes 1048576
  185.1 10.8 %collective-permute-start = (bf16[128,512]{1,0:T(8,128)(2,1)S(1)}, bf16[128,512]{1,0:T(8,128)(2,1)S(1)}, u32[]{:S(2)}, u32[]{:S(2)}) collective-permute-start(bf16[128,512]{1,0:T(8,128)(2,1)S(1)} %dynamic-slice_bitcast_fusion.4), channel_id=1, source_target_pairs={{0,64},{64,128},{128,192},{192,256},{256,320},{320,384},{384,448},... | collective-permute-start | bytes 393224 | tf_op jit(solution)/shard_map/while/body/eval_jaxpr/ppermute | solution.py:18
  197.1 3.4 copy-start.3
  197.1 3.4 copy-start.8
  203.0 7.1 collective-permute-start
  211.4 3.4 copy-start.3
  211.4 3.4 copy-start.8
  217.3 6.9 collective-permute-start
  226.3 9.7 %collective-permute-start = (bf16[128,512]{1,0:T(8,128)(2,1)S(1)}, bf16[128,512]{1,0:T(8,128)(2,1)S(1)}, u32[]{:S(2)}, u32[]{:S(2)}) collective-permute-start(bf16[128,512]{1,0:T(8,128)(2,1)S(1)} %dynamic-slice_bitcast_fusion.4), channel_id=1, source_target_pairs={{0,64},{64,128},{128,192},{192,256},{256,320},{320,384},{384,448},... | collective-permute-start | bytes 393224 | tf_op jit(solution)/shard_map/while/body/eval_jaxpr/ppermute | solution.py:18
  238.2 6.9 collective-permute-start
  247.3 9.4 %collective-permute-start = (bf16[128,512]{1,0:T(8,128)(2,1)S(1)}, bf16[128,512]{1,0:T(8,128)(2,1)S(1)}, u32[]{:S(2)}, u32[]{:S(2)}) collective-permute-start(bf16[128,512]{1,0:T(8,128)(2,1)S(1)} %dynamic-slice_bitcast_fusion.4), channel_id=1, source_target_pairs={{0,64},{64,128},{128,192},{192,256},{256,320},{320,384},{384,448},... | collective-permute-start | bytes 393224 | tf_op jit(solution)/shard_map/while/body/eval_jaxpr/ppermute | solution.py:18
  258.9 6.9 collective-permute-start
  268.0 11.9 %collective-permute-start = (bf16[128,512]{1,0:T(8,128)(2,1)S(1)}, bf16[128,512]{1,0:T(8,128)(2,1)S(1)}, u32[]{:S(2)}, u32[]{:S(2)}) collective-permute-start(bf16[128,512]{1,0:T(8,128)(2,1)S(1)} %dynamic-slice_bitcast_fusion.4), channel_id=1, source_target_pairs={{0,64},{64,128},{128,192},{192,256},{256,320},{320,384},{384,448},... | collective-permute-start | bytes 393224 | tf_op jit(solution)/shard_map/while/body/eval_jaxpr/ppermute | solution.py:18
  282.0 8.1 %collective-permute-start = (bf16[128,512]{1,0:T(8,128)(2,1)S(1)}, bf16[128,512]{1,0:T(8,128)(2,1)S(1)}, u32[]{:S(2)}, u32[]{:S(2)}) collective-permute-start(bf16[128,512]{1,0:T(8,128)(2,1)S(1)} %dynamic-slice_bitcast_fusion.4), channel_id=1, source_target_pairs={{0,64},{64,128},{128,192},{192,256},{256,320},{320,384},{384,448},... | collective-permute-start | bytes 393224 | tf_op jit(solution)/shard_map/while/body/eval_jaxpr/ppermute | solution.py:18
  294.6 8.7 %collective-permute-start.1 = (bf16[128,512]{1,0:T(8,128)(2,1)S(1)}, bf16[128,512]{1,0:T(8,128)(2,1)S(1)}, u32[]{:S(2)}, u32[]{:S(2)}) collective-permute-start(bf16[128,512]{1,0:T(8,128)(2,1)S(1)} %dynamic-slice_bitcast_fusion.5), channel_id=1, source_target_pairs={{64,0},{128,64},{192,128},{256,192},{320,256},{384,320},{448,384},... | collective-permute-start | bytes 393224 | tf_op jit(solution)/shard_map/while/body/eval_jaxpr/ppermute | solution.py:18
  305.4 8.6 %collective-permute-start.1 = (bf16[128,512]{1,0:T(8,128)(2,1)S(1)}, bf16[128,512]{1,0:T(8,128)(2,1)S(1)}, u32[]{:S(2)}, u32[]{:S(2)}) collective-permute-start(bf16[128,512]{1,0:T(8,128)(2,1)S(1)} %dynamic-slice_bitcast_fusion.5), channel_id=1, source_target_pairs={{64,0},{128,64},{192,128},{256,192},{320,256},{384,320},{448,384},... | collective-permute-start | bytes 393224 | tf_op jit(solution)/shard_map/while/body/eval_jaxpr/ppermute | solution.py:18
  316.2 10.6 %collective-permute-start.1 = (bf16[128,512]{1,0:T(8,128)(2,1)S(1)}, bf16[128,512]{1,0:T(8,128)(2,1)S(1)}, u32[]{:S(2)}, u32[]{:S(2)}) collective-permute-start(bf16[128,512]{1,0:T(8,128)(2,1)S(1)} %dynamic-slice_bitcast_fusion.5), channel_id=1, source_target_pairs={{64,0},{128,64},{192,128},{256,192},{320,256},{384,320},{448,384},... | collective-permute-start | bytes 393224 | tf_op jit(solution)/shard_map/while/body/eval_jaxpr/ppermute | solution.py:18
  329.0 8.1 %collective-permute-start.1 = (bf16[128,512]{1,0:T(8,128)(2,1)S(1)}, bf16[128,512]{1,0:T(8,128)(2,1)S(1)}, u32[]{:S(2)}, u32[]{:S(2)}) collective-permute-start(bf16[128,512]{1,0:T(8,128)(2,1)S(1)} %dynamic-slice_bitcast_fusion.5), channel_id=1, source_target_pairs={{64,0},{128,64},{192,128},{256,192},{320,256},{384,320},{448,384},... | collective-permute-start | bytes 393224 | tf_op jit(solution)/shard_map/while/body/eval_jaxpr/ppermute | solution.py:18
  339.2 7.1 collective-permute-start.1
  348.5 58.4 %collective-permute-start.1 = (bf16[128,512]{1,0:T(8,128)(2,1)S(1)}, bf16[128,512]{1,0:T(8,128)(2,1)S(1)}, u32[]{:S(2)}, u32[]{:S(2)}) collective-permute-start(bf16[128,512]{1,0:T(8,128)(2,1)S(1)} %dynamic-slice_bitcast_fusion.5), channel_id=1, source_target_pairs={{64,0},{128,64},{192,128},{256,192},{320,256},{384,320},{448,384},... | collective-permute-start | bytes 393224 | tf_op jit(solution)/shard_map/while/body/eval_jaxpr/ppermute | solution.py:18
  417.7 8.1 %collective-permute-start.1 = (bf16[128,512]{1,0:T(8,128)(2,1)S(1)}, bf16[128,512]{1,0:T(8,128)(2,1)S(1)}, u32[]{:S(2)}, u32[]{:S(2)}) collective-permute-start(bf16[128,512]{1,0:T(8,128)(2,1)S(1)} %dynamic-slice_bitcast_fusion.5), channel_id=1, source_target_pairs={{64,0},{128,64},{192,128},{256,192},{320,256},{384,320},{448,384},... | collective-permute-start | bytes 393224 | tf_op jit(solution)/shard_map/while/body/eval_jaxpr/ppermute | solution.py:18
  436.6 6.9 collective-permute-start.1
  445.7 13.0 %collective-permute-start.1 = (bf16[128,512]{1,0:T(8,128)(2,1)S(1)}, bf16[128,512]{1,0:T(8,128)(2,1)S(1)}, u32[]{:S(2)}, u32[]{:S(2)}) collective-permute-start(bf16[128,512]{1,0:T(8,128)(2,1)S(1)} %dynamic-slice_bitcast_fusion.5), channel_id=1, source_target_pairs={{64,0},{128,64},{192,128},{256,192},{320,256},{384,320},{448,384},... | collective-permute-start | bytes 393224 | tf_op jit(solution)/shard_map/while/body/eval_jaxpr/ppermute | solution.py:18
  458.7 188.8 %copy-start.13 = (f32[1,4,512]{2,1,0:T(4,128)S(1)}, f32[1,4,512]{2,1,0:T(4,128)}, u32[]{:S(2)}) copy-start(f32[1,4,512]{2,1,0:T(4,128)} %param.27) | copy-start | bytes 24580
  458.7 188.8 %copy-start.14 = (f32[1,4,512]{2,1,0:T(4,128)S(1)}, f32[1,4,512]{2,1,0:T(4,128)}, u32[]{:S(2)}) copy-start(f32[1,4,512]{2,1,0:T(4,128)} %param.31) | copy-start | bytes 24580
  458.7 188.8 %copy-start.15 = (f32[1,4,512]{2,1,0:T(4,128)S(1)}, f32[1,4,512]{2,1,0:T(4,128)}, u32[]{:S(2)}) copy-start(f32[1,4,512]{2,1,0:T(4,128)} %param.30) | copy-start | bytes 24580
  458.7 339.6 %copy-start.10 = (f32[1,32,256]{2,1,0:T(8,128)S(1)}, f32[1,32,256]{2,1,0:T(8,128)}, u32[]{:S(2)}) copy-start(f32[1,32,256]{2,1,0:T(8,128)} %param.25) | copy-start | bytes 98308
  458.8 339.6 %copy-start.11 = (f32[1,32,256]{2,1,0:T(8,128)S(1)}, f32[1,32,256]{2,1,0:T(8,128)}, u32[]{:S(2)}) copy-start(f32[1,32,256]{2,1,0:T(8,128)} %param.29) | copy-start | bytes 98308
  458.8 339.6 %copy-start.12 = (f32[1,32,256]{2,1,0:T(8,128)S(1)}, f32[1,32,256]{2,1,0:T(8,128)}, u32[]{:S(2)}) copy-start(f32[1,32,256]{2,1,0:T(8,128)} %param.28) | copy-start | bytes 98308
  459.5 338.8 %reduce-scatter.2.cloned.1.call-start = ((), (), s32[]{:S(2)}) async-start(), calls=%async_computation.2 | async-start | bytes 2129920 | tf_op jit(solution)/shard_map/reduce_scatter | solution.py:187
  (13 other events, 23.4 us)
Sparse Core Ops, SparseCore 0:
  11.9 87.0 all-gather.4
  102.3 79.7 all-gather.6
  459.7 187.8 all-reduce.2
  652.0 146.3 reduce-scatter.1
where the time goes:
time: 808 us; the launch traced here: 806 us
  waiting for transfers between devices  593 us (73%)
  starting transfers between devices  71.7 us (9%)
  blocking collectives  50.3 us (6%)
  local copies, waits for them, and re-layouts  35 us (4%)
  matrix products  19.5 us (2%)
  between operations  14.5 us (2%)
  loops' own time  13 us (2%)
  other arithmetic  9.4 us (1%)
    unnamed x5, waiting for transfers between devices  187 us
    reduce_scatter x1, waiting for transfers between devices, per_device(): lax.psum_scatter(gate_acc, 'replica', scatter_dimension=0, tiled=True)  149 us
    ppermute x18, waiting for transfers between devices, from_behind(): lax.ppermute(value, axis, [(source, source + steps) for source in range(f...  135 us
    all_gather x1, waiting for transfers between devices, per_device(): lax.all_gather(up_weight[0], 'replica', axis=0, tiled=True)  83.1 us
    ppermute x18, starting transfers between devices, from_behind(): lax.ppermute(value, axis, [(source, source + steps) for source in range(f...  71.6 us
    all_gather x1, blocking collectives, per_device(): lax.all_gather(down_weight[0].astype(jnp.bfloat16), 'replica', axis=0, ti...  50.3 us
    all_gather x1, waiting for transfers between devices, per_device(): lax.all_gather(gate_weight[0].astype(jnp.bfloat16), 'replica', axis=0, ti...  38.6 us
  transfers between devices with their start and end apart: 22, of which 22 were waited for; matrix products, arithmetic and copies ran while one was open for 0% of the time, Pallas kernels for 0%

commit v1 on v0

--- a/solution.py
+++ b/solution.py
@@ -10,6 +10,16 @@
 decay_second = 0.95
 step_count = 10
 adam_floor = 1e-08
+
+
+def _apply_numbers(work_x, axis_name, pos_dim):
+    world_n = lax.axis_size(axis_name)
+    local_part = jnp.tile(
+        work_x, tuple((world_n if k0 == pos_dim else 1 for k0 in range(work_x.ndim)))
+    )
+    return lax.all_to_all(
+        local_part, axis_name, split_axis=pos_dim, concat_axis=pos_dim, tiled=True
+    )
 
 
 def from_behind(value, axis, steps):
@@ -104,7 +114,7 @@
     section_index = lax.axis_index("section")
     tick_count = sections + batches - 1
     w_gate, w_up, w_down = (
-        lax.all_gather(gate_weight[0].astype(jnp.bfloat16), "replica", axis=0, tiled=True),
+        _apply_numbers(gate_weight[0].astype(jnp.bfloat16), "replica", 0),
         lax.all_gather(up_weight[0], "replica", axis=0, tiled=True),
         lax.all_gather(down_weight[0].astype(jnp.bfloat16), "replica", axis=0, tiled=True),
     )

time: 808 us -> 805 us (level)
  waiting for transfers between devices: 593 us -> 531 us
  starting transfers between devices: 71.7 us -> 100 us
  local copies, waits for them, and re-layouts: 35 us -> 48.4 us
  blocking collectives: 50.3 us -> 60.2 us
  matrix products: 19.5 us -> 28.2 us
    all_gather x1, waiting for transfers between devices: 83.1 us -> 26.6 us  [per_device(): lax.all_gather(up_weight[0], 'replica', axis=0, tiled=True)]
    all_gather x1 -> x0, waiting for transfers between devices: 38.6 us -> none  [per_device(): lax.all_gather(gate_weight[0].astype(jnp.bfloat16), 'replica', axis=0, ti...]
    ppermute x18, waiting for transfers between devices: 135 us -> 168 us  [from_behind(): lax.ppermute(value, axis, [(source, source + steps) for source in range(f...]
    ppermute x18, starting transfers between devices: 71.6 us -> 86.2 us  [from_behind(): lax.ppermute(value, axis, [(source, source + steps) for source in range(f...]
    all_to_all x0 -> x1, starting transfers between devices: none -> 14 us  [_apply_numbers(): lax.all_to_all(local_part, axis_name, split_axis=pos_dim, concat_axis=pos...]
    all_gather x1, blocking collectives: 50.3 us -> 60.2 us  [per_device(): lax.all_gather(down_weight[0].astype(jnp.bfloat16), 'replica', axis=0, ti...]
    unnamed x5 -> x4, waiting for transfers between devices: 187 us -> 186 us
  transfers between devices with their start and end apart: 22 -> 22, of which waited for: 22 -> 21; matrix products, arithmetic and copies ran while one was open for 0% -> 0% of each run, Pallas kernels for 0% -> 0%
where the time goes in v1:
time: 805 us; the launch traced here: 803 us
  waiting for transfers between devices  531 us (66%)
  starting transfers between devices  100 us (12%)
  blocking collectives  60.2 us (7%)
  local copies, waits for them, and re-layouts  48.4 us (6%)
  matrix products  28.2 us (4%)
  between operations  14.5 us (2%)
  loops' own time  12.9 us (2%)
    unnamed x4, waiting for transfers between devices  186 us
    ppermute x18, waiting for transfers between devices, from_behind(): lax.ppermute(value, axis, [(source, source + steps) for source in range(f...  168 us
    reduce_scatter x1, waiting for transfers between devices, per_device(): lax.psum_scatter(gate_acc, 'replica', scatter_dimension=0, tiled=True)  150 us
    ppermute x18, starting transfers between devices, from_behind(): lax.ppermute(value, axis, [(source, source + steps) for source in range(f...  86.2 us
    all_gather x1, blocking collectives, per_device(): lax.all_gather(down_weight[0].astype(jnp.bfloat16), 'replica', axis=0, ti...  60.2 us
    all_gather x1, waiting for transfers between devices, per_device(): lax.all_gather(up_weight[0], 'replica', axis=0, tiled=True)  26.6 us
  transfers between devices with their start and end apart: 22, of which 21 were waited for; matrix products, arithmetic and copies ran while one was open for 0% of the time, Pallas kernels for 0%

profile of v1, /device:TPU:8, one launch (start us, length us, event | category | flops | bytes accessed | tf_op | source)
XLA Modules:
  0.0 802.6 jit_solution(5700964105219359236)
XLA Ops:
  9.1 14.0 %all-to-all-start = ((bf16[64,32,256]{2,1,0:T(8,128)(2,1)}), bf16[64,32,256]{2,1,0:T(8,128)(2,1)}, u32[]{:S(2)}, u32[]{:S(2)}) async-start(bf16[64,32,256]{2,1,0:T(8,128)(2,1)} %tile.2), calls=%async_computation | async-start | bytes 2097152 | tf_op jit(solution)/shard_map/all_to_all | solution.py:20
  23.9 60.2 %all-gather.1 = bf16[64,4,512]{2,1,0:T(4,128)(2,1)S(1)} all-gather(bf16[1,4,512]{2,1,0:T(4,128)(2,1)S(1)} %fusion.30), channel_id=1, replica_groups=mesh['section'=8,'replica'=64] {'replica'}, dimensions={0}, use_global_device_ids=true | all-gather | bytes 266240 | tf_op jit(solution)/shard_map/all_gather | solution.py:119
  84.2 26.6 %all-gather.4.cloned.1.call-done = bf16[1,2048,256]{2,1,0:T(8,128)(2,1)} async-done(((bf16[1,32,256]{2,1,0:T(8,128)(2,1)}), bf16[1,2048,256]{2,1,0:T(8,128)(2,1)}) %all-gather.4.cloned.1.call-update) | async-done | bytes 1048592 | tf_op jit(solution)/shard_map/all_gather | solution.py:118
  112.3 130.7 %while.33 = (s32[]{:T(128)}, bf16[128,512]{1,0:T(8,128)(2,1)S(1)}, bf16[2,128,512]{2,1,0:T(8,128)(2,1)}, bf16[2,128,512]{2,1,0:T(8,128)(2,1)}, s32[9]{0:T(128)S(...) while((s32[]{:T(128)}, bf16[128,512]{1,0:T(8,128)(2,1)S(1)}, ...), condition=%wide.region_4.5_spmd, body=%wide.region_0.4_spmd.sunk | while | flops 573505664 | bytes 18501632 | solution.py:157
  114.5 3.4 collective-permute-start
  117.9 11.3 %collective-permute-done = bf16[128,512]{1,0:T(8,128)(2,1)S(1)} collective-permute-done((bf16[128,512]{1,0:T(8,128)(2,1)S(1)}, bf16[128,512]{1,0:T(8,128)(2,1)S(1)}, u32[]{:S(2)}, u32[]{:S(2)}) %collective-permute-start) | collective-permute-done | bytes 131104 | tf_op jit(solution)/shard_map/while/body/eval_jaxpr/ppermute | solution.py:28
  130.4 8.9 %conditional.4 = ((bf16[2,128,512]{2,1,0:T(8,128)(2,1)}, bf16[2,128,512]{2,1,0:T(8,128)(2,1)})) conditional(s32[]{:T(128)} %convert_element_type.129, (bf16[2,128,512]{2,1,0:T(8,128)(2,1)}, bf16[2,128,512]{2,1,0:T(8,128)(2,1)}) %tuple.81, (pred[]{:T(512)}, bf16[2,128,512]{2,1,0:T(8,128)(2,1)}, s32[]{:T(128)}, bf16[128,512]{1,0:T(8,128)(2,1)S(1)}, ...), branch_computations={%region_1.1_spmd, %region_2.3_spmd} | conditional | flops 573505664 | bytes 17714814 | solution.py:150
  142.2 5.1 collective-permute-done
  148.6 9.0 %conditional.4 = ((bf16[2,128,512]{2,1,0:T(8,128)(2,1)}, bf16[2,128,512]{2,1,0:T(8,128)(2,1)})) conditional(s32[]{:T(128)} %convert_element_type.129, (bf16[2,128,512]{2,1,0:T(8,128)(2,1)}, bf16[2,128,512]{2,1,0:T(8,128)(2,1)}) %tuple.81, (pred[]{:T(512)}, bf16[2,128,512]{2,1,0:T(8,128)(2,1)}, s32[]{:T(128)}, bf16[128,512]{1,0:T(8,128)(2,1)S(1)}, ...), branch_computations={%region_1.1_spmd, %region_2.3_spmd} | conditional | flops 573505664 | bytes 17714814 | solution.py:150
  160.6 4.7 collective-permute-done
  167.5 11.1 %collective-permute-start = (bf16[128,512]{1,0:T(8,128)(2,1)S(1)}, bf16[128,512]{1,0:T(8,128)(2,1)S(1)}, u32[]{:S(2)}, u32[]{:S(2)}) collective-permute-start(bf16[128,512]{1,0:T(8,128)(2,1)S(1)} %dynamic-slice_bitcast_fusion.4), channel_id=1, source_target_pairs={{0,64},{64,128},{128,192},{192,256},{256,320},{320,384},{384,448},... | collective-permute-start | bytes 393224 | tf_op jit(solution)/shard_map/while/body/eval_jaxpr/ppermute | solution.py:28
  183.3 4.4 collective-permute-start
  192.4 10.8 %collective-permute-start = (bf16[128,512]{1,0:T(8,128)(2,1)S(1)}, bf16[128,512]{1,0:T(8,128)(2,1)S(1)}, u32[]{:S(2)}, u32[]{:S(2)}) collective-permute-start(bf16[128,512]{1,0:T(8,128)(2,1)S(1)} %dynamic-slice_bitcast_fusion.4), channel_id=1, source_target_pairs={{0,64},{64,128},{128,192},{192,256},{256,320},{320,384},{384,448},... | collective-permute-start | bytes 393224 | tf_op jit(solution)/shard_map/while/body/eval_jaxpr/ppermute | solution.py:28
  207.9 4.4 collective-permute-start
  217.0 13.2 %collective-permute-start = (bf16[128,512]{1,0:T(8,128)(2,1)S(1)}, bf16[128,512]{1,0:T(8,128)(2,1)S(1)}, u32[]{:S(2)}, u32[]{:S(2)}) collective-permute-start(bf16[128,512]{1,0:T(8,128)(2,1)S(1)} %dynamic-slice_bitcast_fusion.4), channel_id=1, source_target_pairs={{0,64},{64,128},{128,192},{192,256},{256,320},{320,384},{384,448},... | collective-permute-start | bytes 393224 | tf_op jit(solution)/shard_map/while/body/eval_jaxpr/ppermute | solution.py:28
  234.9 5.6 collective-permute-start
  246.1 210.0 %while.34 = (s32[]{:T(128)}, bf16[128,512]{1,0:T(8,128)(2,1)S(1)}, bf16[2,128,512]{2,1,0:T(8,128)(2,1)}, f32[2048,256]{1,0:T(8,128)}, f32[256,512]{1,0:T(8,128)}...) while((s32[]{:T(128)}, bf16[128,512]{1,0:T(8,128)(2,1)S(1)}, ...), condition=%wide.region_10.11_spmd, body=%wide.region_5.10_spmd.sunk | while | flops 1281163392 | bytes 52255420 | solution.py:191
  250.8 10.9 %collective-permute-done.1 = bf16[128,512]{1,0:T(8,128)(2,1)S(1)} collective-permute-done((bf16[128,512]{1,0:T(8,128)(2,1)}, bf16[128,512]{1,0:T(8,128)(2,1)S(1)}, u32[]{:S(2)}, u32[]{:S(2)}) %collective-permute-start.1) | collective-permute-done | bytes 131104 | tf_op jit(solution)/shard_map/while/body/eval_jaxpr/ppermute | solution.py:28
  266.5 6.8 collective-permute-done.1
  278.0 11.9 %collective-permute-done.1 = bf16[128,512]{1,0:T(8,128)(2,1)S(1)} collective-permute-done((bf16[128,512]{1,0:T(8,128)(2,1)}, bf16[128,512]{1,0:T(8,128)(2,1)S(1)}, u32[]{:S(2)}, u32[]{:S(2)}) %collective-permute-start.1) | collective-permute-done | bytes 131104 | tf_op jit(solution)/shard_map/while/body/eval_jaxpr/ppermute | solution.py:28
  294.7 5.3 collective-permute-done.1
  302.8 2.7 collective-permute-start.1
  305.5 10.5 %collective-permute-done.1 = bf16[128,512]{1,0:T(8,128)(2,1)S(1)} collective-permute-done((bf16[128,512]{1,0:T(8,128)(2,1)}, bf16[128,512]{1,0:T(8,128)(2,1)S(1)}, u32[]{:S(2)}, u32[]{:S(2)}) %collective-permute-start.1) | collective-permute-done | bytes 131104 | tf_op jit(solution)/shard_map/while/body/eval_jaxpr/ppermute | solution.py:28
  320.8 72.8 %collective-permute-done.1 = bf16[128,512]{1,0:T(8,128)(2,1)S(1)} collective-permute-done((bf16[128,512]{1,0:T(8,128)(2,1)}, bf16[128,512]{1,0:T(8,128)(2,1)S(1)}, u32[]{:S(2)}, u32[]{:S(2)}) %collective-permute-start.1) | collective-permute-done | bytes 131104 | tf_op jit(solution)/shard_map/while/body/eval_jaxpr/ppermute | solution.py:28
  394.8 11.3 %conditional.5 = ((bf16[2,128,512]{2,1,0:T(8,128)(2,1)}, f32[2048,256]{1,0:T(8,128)}, f32[256,512]{1,0:T(8,128)})) conditional(s32[]{:T(128)} %convert_element_type.130, (bf16[2,128,512]{2,1,0:T(8,128)(2,1)}, f32[2048,256]{1,0:T(8,128)}, f32[256,512]{1,0:T(8,128)}) %tuple.84, (pred[]{:T(512)}, bf16[2,128,512]{2,1,0:T(8,128)(2,1)}, s32[]{:T(128)}, ...), branch_computations={%region_6.6_spmd, %region_7.9_spmd} | conditional | flops 1281163392 | bytes 51468560 | solution.py:181
  409.7 6.4 collective-permute-done.1
  417.3 11.3 %conditional.5 = ((bf16[2,128,512]{2,1,0:T(8,128)(2,1)}, f32[2048,256]{1,0:T(8,128)}, f32[256,512]{1,0:T(8,128)})) conditional(s32[]{:T(128)} %convert_element_type.130, (bf16[2,128,512]{2,1,0:T(8,128)(2,1)}, f32[2048,256]{1,0:T(8,128)}, f32[256,512]{1,0:T(8,128)}) %tuple.84, (pred[]{:T(512)}, bf16[2,128,512]{2,1,0:T(8,128)(2,1)}, s32[]{:T(128)}, ...), branch_computations={%region_6.6_spmd, %region_7.9_spmd} | conditional | flops 1281163392 | bytes 51468560 | solution.py:181
  432.1 5.1 collective-permute-done.1
  440.1 13.2 %collective-permute-start.1 = (bf16[128,512]{1,0:T(8,128)(2,1)}, bf16[128,512]{1,0:T(8,128)(2,1)S(1)}, u32[]{:S(2)}, u32[]{:S(2)}) collective-permute-start(bf16[128,512]{1,0:T(8,128)(2,1)} %dynamic-slice_bitcast_fusion.5), channel_id=1, source_target_pairs={{64,0},{128,64},{192,128},{256,192},{320,256},{384,320},{448,384},... | collective-permute-start | bytes 393224 | tf_op jit(solution)/shard_map/while/body/eval_jaxpr/ppermute | solution.py:28
  453.3 2.8 collective-permute-done.1
  458.8 184.9 %all-reduce.3.cloned.1.call-done = f32[256,512]{1,0:T(8,128)} async-done(((f32[256,512]{1,0:T(8,128)}), f32[256,512]{1,0:T(8,128)}) %all-reduce.3.cloned.1.call-update) | async-done | bytes 524304
  645.1 149.6 %reduce-scatter.2.cloned.1.call-done = f32[32,256]{1,0:T(8,128)} async-done(((f32[2048,256]{1,0:T(8,128)}), f32[32,256]{1,0:T(8,128)}) %reduce-scatter.2.cloned.1.call-update) | async-done | bytes 32784 | tf_op jit(solution)/shard_map/reduce_scatter | solution.py:197
  (180 shorter events, 117.9 us)
Async XLA Ops:
  7.2 16.7 %copy-start.15 = (f32[1,4,512]{2,1,0:T(4,128)S(1)}, f32[1,4,512]{2,1,0:T(4,128)}, u32[]{:S(2)}) copy-start(f32[1,4,512]{2,1,0:T(4,128)} %param.27) | copy-start | bytes 24580
  7.9 104.3 %copy-start = (bf16[512,2048]{1,0:T(8,128)(2,1)S(1)}, bf16[512,2048]{1,0:T(8,128)(2,1)}, u32[]{:S(2)}) copy-start(bf16[512,2048]{1,0:T(8,128)(2,1)} %param.23) | copy-start | bytes 6291460
  7.9 104.3 %copy-start.8 = (f32[1,2048]{1,0:T(1,128)S(1)}, f32[1,2048]{1,0:T(1,128)}, u32[]{:S(2)}) copy-start(f32[1,2048]{1,0:T(1,128)} %param.24) | copy-start | bytes 24580
  9.1 75.2 %all-to-all-start = ((bf16[64,32,256]{2,1,0:T(8,128)(2,1)}), bf16[64,32,256]{2,1,0:T(8,128)(2,1)}, u32[]{:S(2)}, u32[]{:S(2)}) async-start(bf16[64,32,256]{2,1,0:T(8,128)(2,1)} %tile.2), calls=%async_computation | async-start | bytes 2097152 | tf_op jit(solution)/shard_map/all_to_all | solution.py:20
  23.1 87.7 %all-gather.4.cloned.1.call-start = ((), (), s32[]{:S(2)}) async-start(), calls=%async_computation.3 | async-start | bytes 1064960 | tf_op jit(solution)/shard_map/all_gather | solution.py:118
  23.8 619.8 %all-reduce.3.cloned.1.call-start = ((), (), s32[]{:S(2)}) async-start(), calls=%async_computation.4 | async-start | bytes 1048576
  114.5 14.7 %collective-permute-start = (bf16[128,512]{1,0:T(8,128)(2,1)S(1)}, bf16[128,512]{1,0:T(8,128)(2,1)S(1)}, u32[]{:S(2)}, u32[]{:S(2)}) collective-permute-start(bf16[128,512]{1,0:T(8,128)(2,1)S(1)} %dynamic-slice_bitcast_fusion.4), channel_id=1, source_target_pairs={{0,64},{64,128},{128,192},{192,256},{256,320},{320,384},{384,448},... | collective-permute-start | bytes 393224 | tf_op jit(solution)/shard_map/while/body/eval_jaxpr/ppermute | solution.py:28
  140.2 7.1 collective-permute-start
  150.2 4.9 copy-start.1
  158.4 6.9 collective-permute-start
  167.5 13.6 %collective-permute-start = (bf16[128,512]{1,0:T(8,128)(2,1)S(1)}, bf16[128,512]{1,0:T(8,128)(2,1)S(1)}, u32[]{:S(2)}, u32[]{:S(2)}) collective-permute-start(bf16[128,512]{1,0:T(8,128)(2,1)S(1)} %dynamic-slice_bitcast_fusion.4), channel_id=1, source_target_pairs={{0,64},{64,128},{128,192},{192,256},{256,320},{320,384},{384,448},... | collective-permute-start | bytes 393224 | tf_op jit(solution)/shard_map/while/body/eval_jaxpr/ppermute | solution.py:28
  183.3 6.9 collective-permute-start
  192.4 13.4 %collective-permute-start = (bf16[128,512]{1,0:T(8,128)(2,1)S(1)}, bf16[128,512]{1,0:T(8,128)(2,1)S(1)}, u32[]{:S(2)}, u32[]{:S(2)}) collective-permute-start(bf16[128,512]{1,0:T(8,128)(2,1)S(1)} %dynamic-slice_bitcast_fusion.4), channel_id=1, source_target_pairs={{0,64},{64,128},{128,192},{192,256},{256,320},{320,384},{384,448},... | collective-permute-start | bytes 393224 | tf_op jit(solution)/shard_map/while/body/eval_jaxpr/ppermute | solution.py:28
  207.9 6.9 collective-permute-start
  217.0 15.7 %collective-permute-start = (bf16[128,512]{1,0:T(8,128)(2,1)S(1)}, bf16[128,512]{1,0:T(8,128)(2,1)S(1)}, u32[]{:S(2)}, u32[]{:S(2)}) collective-permute-start(bf16[128,512]{1,0:T(8,128)(2,1)S(1)} %dynamic-slice_bitcast_fusion.4), channel_id=1, source_target_pairs={{0,64},{64,128},{128,192},{192,256},{256,320},{320,384},{384,448},... | collective-permute-start | bytes 393224 | tf_op jit(solution)/shard_map/while/body/eval_jaxpr/ppermute | solution.py:28
  234.9 8.1 %collective-permute-start = (bf16[128,512]{1,0:T(8,128)(2,1)S(1)}, bf16[128,512]{1,0:T(8,128)(2,1)S(1)}, u32[]{:S(2)}, u32[]{:S(2)}) collective-permute-start(bf16[128,512]{1,0:T(8,128)(2,1)S(1)} %dynamic-slice_bitcast_fusion.4), channel_id=1, source_target_pairs={{0,64},{64,128},{128,192},{192,256},{256,320},{320,384},{384,448},... | collective-permute-start | bytes 393224 | tf_op jit(solution)/shard_map/while/body/eval_jaxpr/ppermute | solution.py:28
  248.9 12.8 %collective-permute-start.1 = (bf16[128,512]{1,0:T(8,128)(2,1)}, bf16[128,512]{1,0:T(8,128)(2,1)S(1)}, u32[]{:S(2)}, u32[]{:S(2)}) collective-permute-start(bf16[128,512]{1,0:T(8,128)(2,1)} %dynamic-slice_bitcast_fusion.5), channel_id=1, source_target_pairs={{64,0},{128,64},{192,128},{256,192},{320,256},{384,320},{448,384},... | collective-permute-start | bytes 393224 | tf_op jit(solution)/shard_map/while/body/eval_jaxpr/ppermute | solution.py:28
  264.6 8.7 %collective-permute-start.1 = (bf16[128,512]{1,0:T(8,128)(2,1)}, bf16[128,512]{1,0:T(8,128)(2,1)S(1)}, u32[]{:S(2)}, u32[]{:S(2)}) collective-permute-start(bf16[128,512]{1,0:T(8,128)(2,1)} %dynamic-slice_bitcast_fusion.5), channel_id=1, source_target_pairs={{64,0},{128,64},{192,128},{256,192},{320,256},{384,320},{448,384},... | collective-permute-start | bytes 393224 | tf_op jit(solution)/shard_map/while/body/eval_jaxpr/ppermute | solution.py:28
  276.1 13.9 %collective-permute-start.1 = (bf16[128,512]{1,0:T(8,128)(2,1)}, bf16[128,512]{1,0:T(8,128)(2,1)S(1)}, u32[]{:S(2)}, u32[]{:S(2)}) collective-permute-start(bf16[128,512]{1,0:T(8,128)(2,1)} %dynamic-slice_bitcast_fusion.5), channel_id=1, source_target_pairs={{64,0},{128,64},{192,128},{256,192},{320,256},{384,320},{448,384},... | collective-permute-start | bytes 393224 | tf_op jit(solution)/shard_map/while/body/eval_jaxpr/ppermute | solution.py:28
  292.8 7.2 collective-permute-start.1
  302.8 13.2 %collective-permute-start.1 = (bf16[128,512]{1,0:T(8,128)(2,1)}, bf16[128,512]{1,0:T(8,128)(2,1)S(1)}, u32[]{:S(2)}, u32[]{:S(2)}) collective-permute-start(bf16[128,512]{1,0:T(8,128)(2,1)} %dynamic-slice_bitcast_fusion.5), channel_id=1, source_target_pairs={{64,0},{128,64},{192,128},{256,192},{320,256},{384,320},{448,384},... | collective-permute-start | bytes 393224 | tf_op jit(solution)/shard_map/while/body/eval_jaxpr/ppermute | solution.py:28
  318.9 74.7 %collective-permute-start.1 = (bf16[128,512]{1,0:T(8,128)(2,1)}, bf16[128,512]{1,0:T(8,128)(2,1)S(1)}, u32[]{:S(2)}, u32[]{:S(2)}) collective-permute-start(bf16[128,512]{1,0:T(8,128)(2,1)} %dynamic-slice_bitcast_fusion.5), channel_id=1, source_target_pairs={{64,0},{128,64},{192,128},{256,192},{320,256},{384,320},{448,384},... | collective-permute-start | bytes 393224 | tf_op jit(solution)/shard_map/while/body/eval_jaxpr/ppermute | solution.py:28
  407.7 8.3 %collective-permute-start.1 = (bf16[128,512]{1,0:T(8,128)(2,1)}, bf16[128,512]{1,0:T(8,128)(2,1)S(1)}, u32[]{:S(2)}, u32[]{:S(2)}) collective-permute-start(bf16[128,512]{1,0:T(8,128)(2,1)} %dynamic-slice_bitcast_fusion.5), channel_id=1, source_target_pairs={{64,0},{128,64},{192,128},{256,192},{320,256},{384,320},{448,384},... | collective-permute-start | bytes 393224 | tf_op jit(solution)/shard_map/while/body/eval_jaxpr/ppermute | solution.py:28
  430.2 7.1 collective-permute-start.1
  440.1 16.0 %collective-permute-start.1 = (bf16[128,512]{1,0:T(8,128)(2,1)}, bf16[128,512]{1,0:T(8,128)(2,1)S(1)}, u32[]{:S(2)}, u32[]{:S(2)}) collective-permute-start(bf16[128,512]{1,0:T(8,128)(2,1)} %dynamic-slice_bitcast_fusion.5), channel_id=1, source_target_pairs={{64,0},{128,64},{192,128},{256,192},{320,256},{384,320},{448,384},... | collective-permute-start | bytes 393224 | tf_op jit(solution)/shard_map/while/body/eval_jaxpr/ppermute | solution.py:28
  456.1 187.6 %copy-start.16 = (f32[1,4,512]{2,1,0:T(4,128)S(1)}, f32[1,4,512]{2,1,0:T(4,128)}, u32[]{:S(2)}) copy-start(f32[1,4,512]{2,1,0:T(4,128)} %param.27) | copy-start | bytes 24580
  456.1 187.6 %copy-start.17 = (f32[1,4,512]{2,1,0:T(4,128)S(1)}, f32[1,4,512]{2,1,0:T(4,128)}, u32[]{:S(2)}) copy-start(f32[1,4,512]{2,1,0:T(4,128)} %param.31) | copy-start | bytes 24580
  456.1 187.6 %copy-start.18 = (f32[1,4,512]{2,1,0:T(4,128)S(1)}, f32[1,4,512]{2,1,0:T(4,128)}, u32[]{:S(2)}) copy-start(f32[1,4,512]{2,1,0:T(4,128)} %param.30) | copy-start | bytes 24580
  456.1 338.6 %copy-start.12 = (f32[1,32,256]{2,1,0:T(8,128)S(1)}, f32[1,32,256]{2,1,0:T(8,128)}, u32[]{:S(2)}) copy-start(f32[1,32,256]{2,1,0:T(8,128)} %param.25) | copy-start | bytes 98308
  456.1 338.6 %copy-start.13 = (f32[1,32,256]{2,1,0:T(8,128)S(1)}, f32[1,32,256]{2,1,0:T(8,128)}, u32[]{:S(2)}) copy-start(f32[1,32,256]{2,1,0:T(8,128)} %param.29) | copy-start | bytes 98308
  456.1 338.5 %copy-start.14 = (f32[1,32,256]{2,1,0:T(8,128)S(1)}, f32[1,32,256]{2,1,0:T(8,128)}, u32[]{:S(2)}) copy-start(f32[1,32,256]{2,1,0:T(8,128)} %param.28) | copy-start | bytes 98308
  456.2 338.5 %reduce-scatter.2.cloned.1.call-start = ((), (), s32[]{:S(2)}) async-start(), calls=%async_computation.2 | async-start | bytes 2129920 | tf_op jit(solution)/shard_map/reduce_scatter | solution.py:197
  (18 other events, 29.2 us)
Sparse Core Ops, SparseCore 0:
  27.3 83.4 all-gather.3
  456.3 187.3 all-reduce.2
  648.3 146.2 reduce-scatter.1
